TPU v7x, 256 devices: a whole 4x4x8 slice. The times are simulated.
256 devices in a mesh: leaf: 16 (over x_hi, z), blk: 4 (over x_lo, core), kv: 4 (over y).
Axes of the slice: x: 4 (x_hi: 2, x_lo: 2; x = x_hi * 2 + x_lo), y: 4, z: 8, core: 2. Of those that a mesh axis runs over, the one named last changes fastest.
Arguments:
- queries: bfloat16 [32768, 2560], P(('leaf', 'blk', 'kv')), parts along dimension 0, may hold values from -8 to 8
- keys: bfloat16 [131072, 512], P(('leaf', 'blk', 'kv')), parts along dimension 0, may hold values from -8 to 8
- values: bfloat16 [131072, 512], P(('leaf', 'blk', 'kv')), parts along dimension 0, may hold values from -6 to 6
- ancestry: int32 [256, 64], P('leaf'), parts along dimension 0, may hold values from 0 to 1, as said below
- leaf_tiles: int32 [256], P('leaf'), parts along dimension 0, may hold values from 1 to 63, as said below
Outputs:
- attended: bfloat16 [32768, 2560], P(('leaf', 'blk', 'kv')), parts along dimension 0
There are 16 independent parts, one for each index of `leaf`. A program takes and returns all parts, laid end to end along the dimension named above; each array names one. Nothing has to cross between parts.
Inputs may be any that keep to these rules, and one draw needn't show every extreme that they name: ancestry[a, t] is 1 exactly when key tile t is a strict ancestor of tile leaf_tiles[a] in the tree whose nodes are the key tiles; tile 0 is the root of the tree. `leaf_tiles`: strictly rising; the last entry is 63.
All inputs are finite; a program needn't handle non-finite values.
Results may differ from a plain program's by a relative error of at most 0.018.
Values may be sent and summed in bfloat16 or wider, within the bound.
No kernel may reach another device: no remote copies, remote signals or barrier semaphores. Data moves between devices by JAX's collectives and lax.ppermute only.
A program may use at most 256 MiB of HBM per device.

v0:
```python
import math

import jax
import jax.numpy as jnp
from jax import lax
from jax.sharding import PartitionSpec as P

TILE = 128
KV_HEADS = 4
GROUP = 5
DH = 128


def row_tables(ancestry, leaf_tiles, first_row, row_count):
    query_ids = first_row + jnp.arange(row_count, dtype=jnp.int32)
    query_tiles = query_ids // TILE
    picker = (
        query_tiles[:, None] == jnp.arange(ancestry.shape[0], dtype=jnp.int32)[None, :]
    ).astype(jnp.float32)
    tile_rows = jnp.dot(picker, ancestry.astype(jnp.float32), precision=lax.Precision.HIGHEST)
    home_tile = jnp.dot(picker, leaf_tiles.astype(jnp.float32), precision=lax.Precision.HIGHEST)
    return (tile_rows, home_tile, query_ids % TILE)


def key_mask(tables, key_ids):
    tile_rows, home_tile, in_tile = tables
    key_tiles = key_ids // TILE
    picker = (
        key_tiles[:, None] == jnp.arange(tile_rows.shape[1], dtype=jnp.int32)[None, :]
    ).astype(jnp.float32)
    linked = jnp.dot(tile_rows, picker.T, precision=lax.Precision.HIGHEST) > 0.5
    own_tile = key_tiles.astype(jnp.float32)[None, :] == home_tile[:, None]
    causal = (key_ids % TILE)[None, :] <= in_tile[:, None]
    return jnp.where(own_tile, causal, linked)


def attend(carried, query_heads, key_piece, value_piece, allowed):
    row_peak, row_total, summed = carried
    scaling = 1.0 / math.sqrt(DH)
    key_heads = key_piece.reshape(key_piece.shape[0], KV_HEADS, DH)
    value_heads = value_piece.reshape(value_piece.shape[0], KV_HEADS, DH)
    scores = (
        jnp.einsum("qhgd,khd->hgqk", query_heads, key_heads, preferred_element_type=jnp.float32)
        * scaling
    )
    scores = jnp.where(allowed[None, None], scores, -1e30)
    new_peak = jnp.maximum(row_peak, jnp.max(scores, axis=-1))
    weights = jnp.where(allowed[None, None], jnp.exp(scores - new_peak[..., None]), 0.0)
    row_total = jnp.sum(weights, axis=-1)
    update = jnp.einsum(
        "hgqk,khd->qhgd",
        weights.astype(jnp.bfloat16),
        value_heads,
        preferred_element_type=jnp.float32,
    )
    summed = update
    return (new_peak, row_total, summed)


def block_step(tables, query_heads, key_ids_of, carried, pieces, offset):
    key_piece, value_piece = pieces
    allowed = key_mask(tables, key_ids_of(offset, key_piece.shape[0]))
    return attend(carried, query_heads, key_piece, value_piece, allowed)


def starting(row_count):
    return (
        jnp.full((KV_HEADS, GROUP, row_count), -1e30, jnp.float32),
        jnp.zeros((KV_HEADS, GROUP, row_count), jnp.float32),
        jnp.zeros((row_count, KV_HEADS, GROUP, DH), jnp.float32),
    )


def finish(row_total, summed):
    result = summed / jnp.transpose(row_total, (2, 0, 1))[..., None]
    return result.reshape(result.shape[0], KV_HEADS * GROUP * DH).astype(jnp.bfloat16)


def on_device(queries, keys, values, ancestry, leaf_tiles):
    own_rows = queries.shape[0]
    first_row = lax.axis_index(("blk", "kv")) * own_rows
    tables = row_tables(ancestry, leaf_tiles, first_row, own_rows)
    query_heads = queries.reshape(own_rows, KV_HEADS, GROUP, DH)

    def whole_ids(offset, length):
        return jnp.arange(length, dtype=jnp.int32)

    result = block_step(
        tables,
        query_heads,
        whole_ids,
        starting(own_rows),
        (
            lax.all_gather(keys, ("blk", "kv"), axis=0, tiled=True),
            lax.all_gather(values, ("blk", "kv"), axis=0, tiled=True),
        ),
        jnp.int32(0),
    )
    return finish(result[1], result[2])


def solution(mesh):
    in_specs = (
        P(("leaf", "blk", "kv"), None),
        P(("leaf", "blk", "kv"), None),
        P(("leaf", "blk", "kv"), None),
        P("leaf", None),
        P("leaf"),
    )
    out_specs = P(("leaf", "blk", "kv"), None)
    return jax.shard_map(
        on_device, mesh=mesh, in_specs=in_specs, out_specs=out_specs, check_vma=False
    )
```

profile of v0, /device:TPU:2, one launch (start us, length us, event | category | flops | bytes accessed | tf_op | source)
XLA Modules:
  0.0 184.3 jit_solution(4825969488345537671)
XLA Ops:
  6.5 0.0 all-gather.3.cloned.1.call-start
  6.5 2.0 %copy.20 = bf16[512,512]{0,1:T(8,128)(2,1)} copy(bf16[512,512]{1,0:T(8,128)(2,1)} %param.6) | data formatting | bytes 1048576 | tf_op args[1]
  8.6 0.0 all-gather.3.cloned.1.call-update
  8.6 0.0 all-gather.5.cloned.1.call-start
  8.7 0.7 all-gather.5.cloned.1.call-update
  9.4 0.8 convolution_bitcast_fusion
  10.2 0.1 fusion.14
  10.3 1.0 fusion.13
  11.3 2.8 %fusion.6 = pred[128,8192]{1,0:T(8,128)(4,1)S(1)} fusion(f32[128,64]{0,1:T(8,128)S(1)} %fusion.13, s32[8192]{0:T(1024)S(1)} %get-tuple-element.9, f32[8192]{0:T(1024)S(1)} %fusion.23, s32[128]{0:T(128)S(1)} %get-tuple-element.7, f32[128]{0:T(128)S(1)} %convolution_bitcast_fusion, s32[8192]{0:T(1024)S(1)} %get-tuple-element.10), kind=kOutput, calls=%fused_computation.8 | convolution fusion | flops 810024960 | bytes 1180672 | tf_op jit(solution)/shard_map/dot_general | solution.py:31
  14.1 2.5 %copy.19 = pred[128,8192]{0,1:T(8,128)(4,1)S(1)} copy(pred[128,8192]{1,0:T(8,128)(4,1)S(1)} %fusion.6) | data formatting | bytes 2097152 | tf_op jit(solution)/shard_map/jit(_where)/select_n | solution.py:34
  16.6 1.4 copy.21
  18.0 51.9 %all-gather.3.cloned.1.call-done = bf16[8192,512]{0,1:T(8,128)(2,1)} async-done(((bf16[512,512]{0,1:T(8,128)(2,1)}), bf16[8192,512]{0,1:T(8,128)(2,1)}) %all-gather.3.cloned.1.call-update) | async-done | bytes 8388624 | tf_op jit(solution)/shard_map/all_gather | solution.py:94
  70.0 33.4 %fusion = (f32[4,5,128]{2,1,0:T(8,128)S(1)}, f32[4,8192,128,5]{2,1,3,0:T(8,128)}) fusion(pred[128,8192]{0,1:T(8,128)(4,1)S(1)} %copy.19, bf16[8192,4,128,1]{0,2,3,1:T(8,128)(2,1)} %bitcast.45, bf16[128,4,5,128]{0,3,2,1:T(8,128)(2,1)S(1)} %bitcast.42), kind=kOutput, calls=%fused_computation.2 | convolution fusion | flops 5431621120 | bytes 93988864 | tf_op jit(solution)/shard_map/qhgd,khd->hgqk/dot_general | solution.py:43
  103.4 27.7 %fusion.1 = f32[4,5,128]{2,1,0:T(8,128)S(1)} fusion(f32[4,8192,128,5]{2,1,3,0:T(8,128)} %get-tuple-element.6, f32[4,5,128]{2,1,0:T(8,128)S(1)} %broadcast_maximum_fusion, pred[128,8192]{0,1:T(8,128)(4,1)S(1)} %copy.19), kind=kLoop, calls=%fused_computation.3 | loop fusion | flops 104855040 | bytes 84955136 | tf_op jit(solution)/shard_map/reduce_sum | solution.py:49
  131.1 0.1 all-gather.5.cloned.1.call-done
  131.1 12.0 %copy.24 = bf16[8192,512]{0,1:T(8,128)(2,1)} copy(bf16[8192,512]{1,0:T(8,128)(2,1)} %all-gather.5.cloned.1.call-done) | data formatting | bytes 16777216 | tf_op jit(solution)/shard_map/all_gather | solution.py:95
  143.2 33.2 %divide_convert_fusion = bf16[128,4,5,128]{0,3,2,1:T(8,128)(2,1)S(1)} fusion(bf16[8192,4,128,1]{0,2,3,1:T(8,128)(2,1)} %bitcast.41, f32[4,8192,128,5]{2,1,3,0:T(8,128)} %get-tuple-element.6, f32[4,5,128]{2,1,0:T(8,128)S(1)} %broadcast_maximum_fusion, pred[128,8192]{0,1:T(8,128)(4,1)S(1)} %copy.19, f32[128,4,5]{0,2,1:T(8,128)S(1)} %bitcast.44), kind=kOutput, calls=%fused_computation.11 | convolution fusion | flops 5474222080 | bytes 93999104 | tf_op jit(solution)/shard_map/hgqk,khd->qhgd/dot_general | solution.py:50
  176.3 1.1 copy.26
  (3 shorter events, 0.0 us)
Async XLA Ops:
  6.5 63.4 %all-gather.3.cloned.1.call-start = ((), (), s32[]{:S(2)}) async-start(), calls=%async_computation | async-start | bytes 8912896 | tf_op jit(solution)/shard_map/all_gather | solution.py:94
  8.6 122.5 %all-gather.5.cloned.1.call-start = ((), (), s32[]{:S(2)}) async-start(), calls=%async_computation.1 | async-start | bytes 8912896 | tf_op jit(solution)/shard_map/all_gather | solution.py:95
Sparse Core Ops, SparseCore 0:
  9.2 60.7 all-gather.2
  71.8 59.3 all-gather.4
where the time goes:
time: 186 us; the launch traced here: 184 us
  matrix products  71.2 us (38%)
  waiting for transfers between devices  52.7 us (28%)
  other arithmetic  27.8 us (15%)
  local copies, waits for them, and re-layouts  19 us (10%)
  between operations  13.5 us (7%)
    all_gather x1, waiting for transfers between devices, on_device(): lax.all_gather(keys, ('blk', 'kv'), axis=0, tiled=True)  51.9 us
    dot_general x1, matrix products, attend(): jnp.einsum('qhgd,khd->hgqk', query_heads, key_heads, preferred_element_ty...  33.4 us
    dot_general x1, matrix products, attend(): jnp.einsum('hgqk,khd->qhgd', weights.astype(jnp.bfloat16), value_heads, p...  33.2 us
    reduce_sum x1, other arithmetic, attend(): row_total = jnp.sum(weights, axis=-1)  27.7 us
    all_gather x1, local copies, waits for them, and re-layouts, on_device(): lax.all_gather(values, ('blk', 'kv'), axis=0, tiled=True)  12 us
  transfers between devices with their start and end apart: 2, of which 2 were waited for; matrix products, arithmetic and copies ran while one was open for 38% of the time, Pallas kernels for 0%

commit v1 on v0

v1 whole, which is shorter than its diff:
```python
import functools
import math

import jax
import jax.numpy as jnp
from jax import lax
from jax.experimental import pallas as pl
from jax.experimental.pallas import tpu as pltpu
from jax.sharding import PartitionSpec as P

TILE = 128
KV_HEADS = 4
GROUP = 5
DH = 128
WIDE = GROUP * DH
RING = 4
BLKS = 4
LOW = -1e30
SCALE = math.log2(math.e) / math.sqrt(DH)


def pack_kernel(q_ref, k_ref, v_ref, *refs):
    kv_out, q_out = refs[:RING], refs[RING:]
    me = lax.axis_index("kv")
    for step in range(RING):
        head = lax.rem(me + step, RING)
        narrow = pl.ds(pl.multiple_of(head * DH, DH), DH)
        wide = pl.ds(pl.multiple_of(head * WIDE, DH), WIDE)
        kv_out[step][0] = k_ref[:, narrow]
        kv_out[step][1] = v_ref[:, narrow]
        q_out[step][...] = q_ref[:, wide]


def pack(queries, keys, values):
    rows = keys.shape[0]
    vmem = pl.BlockSpec(memory_space=pltpu.VMEM)
    return pl.pallas_call(
        pack_kernel,
        out_shape=[jax.ShapeDtypeStruct((2, rows, DH), jnp.bfloat16)] * RING
        + [jax.ShapeDtypeStruct((TILE, WIDE), jnp.bfloat16)] * RING,
        in_specs=[vmem] * 3,
        out_specs=[vmem] * (2 * RING),
        name="pack",
    )(queries, keys, values)


def unpack_kernel(*refs):
    parts, out_ref = refs[:RING], refs[RING]
    me = lax.axis_index("kv")
    for step in range(RING):
        head = lax.rem(me + step, RING)
        wide = pl.ds(pl.multiple_of(head * WIDE, DH), WIDE)
        out_ref[:, wide] = parts[step][...]


def unpack(parts):
    vmem = pl.BlockSpec(memory_space=pltpu.VMEM)
    return pl.pallas_call(
        unpack_kernel,
        out_shape=jax.ShapeDtypeStruct((TILE, KV_HEADS * WIDE), jnp.bfloat16),
        in_specs=[vmem] * RING,
        out_specs=vmem,
        name="unpack",
    )(*parts)


def attend_kernel(slots_ref, counts_ref, *refs):
    q_refs, kv_refs = refs[:RING], refs[RING : RING + RING * BLKS]
    o_refs = refs[RING + RING * BLKS : 2 * RING + RING * BLKS]
    held, scores, sems = refs[2 * RING + RING * BLKS :]
    copies = [
        pltpu.make_async_copy(kv_refs[i], held.at[i], sems.at[i]) for i in range(RING * BLKS)
    ]
    for copy in copies:
        copy.start()
    for copy in copies:
        copy.wait()
    tiles_each = held.shape[2] // TILE
    ahead = lax.broadcasted_iota(jnp.int32, (TILE, TILE), 1) - lax.broadcasted_iota(
        jnp.int32, (TILE, TILE), 0
    )

    def tile_of(which, slot):
        block = slot // tiles_each
        row = pl.multiple_of((slot % tiles_each) * TILE, TILE)
        return held[block, which, pl.ds(row, TILE), :]

    def pair_of(which, step, pair):
        return jnp.concatenate(
            [tile_of(which, slots_ref[step, 2 * pair]), tile_of(which, slots_ref[step, 2 * pair + 1])], axis=0
        )

    for step in range(RING):
        count = counts_ref[step]
        pairs = (count + 1) // 2
        queries = jnp.concatenate(
            [q_refs[step][:, g * DH : (g + 1) * DH] for g in range(GROUP)], axis=0
        )

        def reach(tile):
            return jnp.where(tile < count - 1, TILE, jnp.where(tile == count - 1, 0, -TILE))

        def first(pair, peak):
            keys = pair_of(0, step, pair)
            raw = lax.dot_general(
                queries, keys, (((1,), (1,)), ((), ())), preferred_element_type=jnp.float32
            )
            for half in range(2):
                allowed = ahead <= reach(2 * pair + half)
                part = raw[:, half * TILE : (half + 1) * TILE].reshape(GROUP, TILE, TILE)
                part = jnp.where(allowed[None], part, LOW).reshape(GROUP * TILE, TILE)
                scores[pair, :, half * TILE : (half + 1) * TILE] = part
                peak = jnp.maximum(peak, part)
            return peak

        peak = lax.fori_loop(0, pairs, first, jnp.full((GROUP * TILE, TILE), LOW, jnp.float32))
        peak = jnp.max(peak, axis=1, keepdims=True) * SCALE

        def second(pair, carried):
            total, summed = carried
            weights = jnp.exp2(scores[pair] * SCALE - peak)
            total = total + weights[:, :TILE] + weights[:, TILE:]
            summed = summed + jnp.dot(
                weights.astype(jnp.bfloat16), pair_of(1, step, pair), preferred_element_type=jnp.float32
            )
            return (total, summed)

        zero = jnp.zeros((GROUP * TILE, TILE), jnp.float32)
        total, summed = lax.fori_loop(0, pairs, second, (zero, zero))
        result = (summed / jnp.sum(total, axis=1, keepdims=True)).astype(jnp.bfloat16)
        for g in range(GROUP):
            o_refs[step][:, g * DH : (g + 1) * DH] = result[g * TILE : (g + 1) * TILE]


def attend(slots, counts, query_parts, kv_parts, key_tiles):
    rows = kv_parts[0].shape[1]
    vmem = pl.BlockSpec(memory_space=pltpu.VMEM)
    smem = pl.BlockSpec(memory_space=pltpu.SMEM)
    return pl.pallas_call(
        attend_kernel,
        out_shape=[jax.ShapeDtypeStruct((TILE, WIDE), jnp.bfloat16)] * RING,
        in_specs=[smem, smem] + [vmem] * RING + [pl.BlockSpec(memory_space=pl.ANY)] * (RING * BLKS),
        out_specs=[vmem] * RING,
        scratch_shapes=[
            pltpu.VMEM((RING * BLKS, 2, rows, DH), jnp.bfloat16),
            pltpu.VMEM(((key_tiles + 1) // 2, GROUP * TILE, 2 * TILE), jnp.float32),
            pltpu.SemaphoreType.DMA((RING * BLKS,)),
        ],
        compiler_params=pltpu.CompilerParams(vmem_limit_bytes=44 * 1024 * 1024),
        cost_estimate=pl.CostEstimate(flops=10**9, bytes_accessed=6 * 10**6, transcendentals=10**6),
        name="attend",
    )(slots, counts, *query_parts, *kv_parts)


def chain_lists(ancestry, leaf_tiles, blk, me):
    tiles = ancestry.shape[1]
    each = tiles // (BLKS * RING)
    rows = blk * RING + (me - jnp.arange(RING, dtype=jnp.int32)) % RING
    picker = rows[:, None] == jnp.arange(ancestry.shape[0], dtype=jnp.int32)[None, :]
    linked = jnp.sum(jnp.where(picker[:, :, None], ancestry[None], 0), axis=1)
    home = jnp.sum(jnp.where(picker, leaf_tiles[None], 0), axis=1)
    tile = jnp.arange(tiles, dtype=jnp.int32)
    owner = tile // each
    place = (((owner // RING) ^ blk) * RING + (me - owner) % RING) * each + tile % each
    counts = jnp.sum(linked, axis=1)
    lower = tile[:, None] < tile[None, :]
    rank = jnp.sum(jnp.where(lower[None], linked[:, :, None], 0), axis=1)
    hit = (linked[:, :, None] == 1) & (rank[:, :, None] == tile[None, None, :])
    slots = jnp.sum(jnp.where(hit, place[None, :, None], 0), axis=1)
    own = jnp.sum(jnp.where(home[:, None] == tile[None, :], place[None], 0), axis=1)
    slots = jnp.where(tile[None, :] == counts[:, None], own[:, None], slots)
    return slots.astype(jnp.int32), (counts + 1).astype(jnp.int32)


def turn(array, by):
    return lax.ppermute(array, "kv", [(i, (i + by) % RING) for i in range(RING)])


def across(array, bit):
    return lax.ppermute(array, "blk", [(i, i ^ bit) for i in range(BLKS)])


def on_device(queries, keys, values, ancestry, leaf_tiles):
    me = lax.axis_index("kv")
    blk = lax.axis_index("blk")
    packed = pack(queries, keys, values)
    kv_sent, q_sent = packed[:RING], packed[RING:]
    slots, counts = chain_lists(ancestry, leaf_tiles, blk, me)
    own = [kv_sent[0], None, None, None]
    order = (0, 1, 3, 2)
    for step in order[1:]:
        own[step] = turn(kv_sent[step], step)
    far = [None] * RING
    for step in order:
        far[step] = across(own[step], 2)
    q_parts = [q_sent[0]] + [turn(q_sent[step], step) for step in range(1, RING)]
    near = [across(part, 1) for part in own]
    diagonal = [across(part, 1) for part in far]
    outs = attend(slots, counts, q_parts, own + near + far + diagonal, ancestry.shape[1])
    back = [outs[0]] + [turn(outs[step], -step) for step in range(1, RING)]
    return unpack(back)


def solution(mesh):
    in_specs = (
        P(("leaf", "blk", "kv"), None),
        P(("leaf", "blk", "kv"), None),
        P(("leaf", "blk", "kv"), None),
        P("leaf", None),
        P("leaf"),
    )
    out_specs = P(("leaf", "blk", "kv"), None)
    return jax.shard_map(
        on_device, mesh=mesh, in_specs=in_specs, out_specs=out_specs, check_vma=False
    )
```

time: 186 us -> 82.1 us (0.44)
  matrix products: 71.2 us -> 0 us
  other arithmetic: 27.8 us -> 1.06 us
  Pallas kernels: 0 us -> 17 us
  local copies, waits for them, and re-layouts: 19 us -> 3.81 us
  starting transfers between devices: 0.04 us -> 14.9 us
  between operations: 13.5 us -> 0.09 us
  waiting for transfers between devices: 52.7 us -> 43.9 us
    dot_general x5 -> x0, matrix products: 71.2 us -> none  [the longest x1 33.4 us: attend(): jnp.einsum('qhgd,khd->hgqk', query_heads, key_heads, preferred_element_ty...]
    all_gather x2 -> x0, waiting for transfers between devices: 52 us -> none  [the longest x1 51.9 us: on_device(): lax.all_gather(keys, ('blk', 'kv'), axis=0, tiled=True)]
    ppermute x0 -> x21, waiting for transfers between devices: none -> 43.9 us  [the longest x9 28.1 us: turn(): lax.ppermute(array, 'kv', [(i, (i + by) % RING) for i in range(RING)])]
    reduce_sum x1 -> x5, other arithmetic: 27.7 us -> 0.87 us  [the longest x1 0.24 us: chain_lists(): counts = jnp.sum(linked, axis=1)]
    pallas_call x0 -> x3, Pallas kernels: none -> 17 us  [the longest x1 12.2 us: attend(): pl.pallas_call(attend_kernel, out_shape=[jax.ShapeDtypeStruct((TILE, WIDE...]
    ppermute x0 -> x21, starting transfers between devices: none -> 14.9 us  [the longest x9 9.44 us: turn(): lax.ppermute(array, 'kv', [(i, (i + by) % RING) for i in range(RING)])]
    all_gather x1 -> x0, local copies, waits for them, and re-layouts: 12 us -> none  [on_device(): lax.all_gather(values, ('blk', 'kv'), axis=0, tiled=True)]
    select_n x1 -> x0, local copies, waits for them, and re-layouts: 2.49 us -> none  [key_mask(): return jnp.where(own_tile, causal, linked)]
  transfers between devices with their start and end apart: 2 -> 21, of which waited for: 2 -> 10; matrix products, arithmetic and copies ran while one was open for 38% -> 1% of each run, Pallas kernels for 0% -> 0%
where the time goes in v1:
time: 82.1 us; the launch traced here: 80.8 us
  waiting for transfers between devices  43.9 us (53%)
  Pallas kernels  17 us (21%)
  starting transfers between devices  14.9 us (18%)
  local copies, waits for them, and re-layouts  3.81 us (5%)
  other arithmetic  1.06 us (1%)
    ppermute x9, waiting for transfers between devices, turn(): lax.ppermute(array, 'kv', [(i, (i + by) % RING) for i in range(RING)])  28.1 us
    ppermute x12, waiting for transfers between devices, across(): return lax.ppermute(array, 'blk', [(i, i ^ bit) for i in range(BLKS)])  15.8 us
    pallas_call x1, Pallas kernels, attend(): pl.pallas_call(attend_kernel, out_shape=[jax.ShapeDtypeStruct((TILE, WIDE...  12.2 us
    ppermute x9, starting transfers between devices, turn(): lax.ppermute(array, 'kv', [(i, (i + by) % RING) for i in range(RING)])  9.44 us
    ppermute x12, starting transfers between devices, across(): return lax.ppermute(array, 'blk', [(i, i ^ bit) for i in range(BLKS)])  5.42 us
    unnamed x16, local copies, waits for them, and re-layouts  3.81 us
    pallas_call x1, Pallas kernels, pack(): pl.pallas_call(pack_kernel, out_shape=[jax.ShapeDtypeStruct((2, rows, DH)...  2.79 us
    pallas_call x1, Pallas kernels, unpack(): pl.pallas_call(unpack_kernel, out_shape=jax.ShapeDtypeStruct((TILE, KV_HE...  2.06 us
  transfers between devices with their start and end apart: 21, of which 10 were waited for; matrix products, arithmetic and copies ran while one was open for 1% of the time, Pallas kernels for 0%

profile of v1, /device:TPU:2, one launch (start us, length us, event | category | flops | bytes accessed | tf_op | source)
XLA Modules:
  0.0 80.8 jit_solution(17698282403129827816)
XLA Ops:
  0.0 2.8 %pack.1 = (bf16[2,512,128]{2,1,0:T(8,128)(2,1)}, bf16[2,512,128]{2,1,0:T(8,128)(2,1)}, bf16[2,512,128]{2,1,0:T(8,128)(2,1)}, bf16[2,512,128]{2,1,0:T(8,128)(2,1)...) custom-call(bf16[128,2560]{1,0:T(8,128)(2,1)} %q_ref.1, ...), custom_call_target="tpu_custom_call" | custom-call | tf_op jit(solution)/shard_map/pack/pallas_call | solution.py:37
  2.8 2.3 %collective-permute-start.10 = (bf16[2,512,128]{2,1,0:T(8,128)(2,1)}, bf16[2,512,128]{2,1,0:T(8,128)(2,1)S(1)}, u32[]{:S(2)}, u32[]{:S(2)}) collective-permute-start(bf16[2,512,128]{2,1,0:T(8,128)(2,1)} %get-tuple-element.21.refs_4_), channel_id=1, source_target_pairs={{0,8},{4,12},{8,0},{12,4},{1,9},{5,13},{9,1},{13,5},{2,10},{6,14},... | collective-permute-start | bytes 786440 | tf_op jit(solution)/shard_map/ppermute | solution.py:180
  5.1 2.7 %collective-permute-start.1 = (bf16[128,640]{1,0:T(8,128)(2,1)}, bf16[128,640]{1,0:T(8,128)(2,1)S(1)}, u32[]{:S(2)}, u32[]{:S(2)}) collective-permute-start(bf16[128,640]{1,0:T(8,128)(2,1)} %get-tuple-element.19), channel_id=1, source_target_pairs={{0,2},{1,3},{2,0},{3,1},{4,6},{5,7},{6,4},{7,5},{8,10},{9,11},{10,... | collective-permute-start | bytes 491528 | tf_op jit(solution)/shard_map/ppermute | solution.py:176
  7.8 1.3 %collective-permute-start.2 = (bf16[128,640]{1,0:T(8,128)(2,1)}, bf16[128,640]{1,0:T(8,128)(2,1)S(1)}, u32[]{:S(2)}, u32[]{:S(2)}) collective-permute-start(bf16[128,640]{1,0:T(8,128)(2,1)} %get-tuple-element.20), channel_id=1, source_target_pairs={{0,3},{1,0},{2,1},{3,2},{4,7},{5,4},{6,5},{7,6},{8,11},{9,8},{10,9... | collective-permute-start | bytes 491528 | tf_op jit(solution)/shard_map/ppermute | solution.py:176
  9.2 0.6 copy-done.6
  9.9 0.2 select_reduce_fusion.3
  10.1 6.5 %collective-permute-done.refs_1_ = bf16[128,640]{1,0:T(8,128)(2,1)S(1)} collective-permute-done((bf16[128,640]{1,0:T(8,128)(2,1)}, bf16[128,640]{1,0:T(8,128)(2,1)S(1)}, u32[]{:S(2)}, u32[]{:S(2)}) %collective-permute-start) | collective-permute-done | bytes 163872 | tf_op jit(solution)/shard_map/ppermute | solution.py:176
  16.6 1.0 %collective-permute-start.4 = (bf16[2,512,128]{2,1,0:T(8,128)(2,1)}, bf16[2,512,128]{2,1,0:T(8,128)(2,1)S(1)}, u32[]{:S(2)}, u32[]{:S(2)}) collective-permute-start(bf16[2,512,128]{2,1,0:T(8,128)(2,1)} %get-tuple-element.23), channel_id=1, source_target_pairs={{0,2},{1,3},{2,0},{3,1},{4,6},{5,7},{6,4},{7,5},{8,10},{9,11},{10,... | collective-permute-start | bytes 786440 | tf_op jit(solution)/shard_map/ppermute | solution.py:176
  17.7 2.3 %collective-permute-start.5 = (bf16[2,512,128]{2,1,0:T(8,128)(2,1)}, bf16[2,512,128]{2,1,0:T(8,128)(2,1)S(1)}, u32[]{:S(2)}, u32[]{:S(2)}) collective-permute-start(bf16[2,512,128]{2,1,0:T(8,128)(2,1)} %get-tuple-element.24), channel_id=1, source_target_pairs={{0,3},{1,0},{2,1},{3,2},{4,7},{5,4},{6,5},{7,6},{8,11},{9,8},{10,9... | collective-permute-start | bytes 786440 | tf_op jit(solution)/shard_map/ppermute | solution.py:176
  20.1 0.2 select_reduce_fusion
  20.2 11.0 %collective-permute-done.3.refs_5_ = bf16[2,512,128]{2,1,0:T(8,128)(2,1)S(1)} collective-permute-done((bf16[2,512,128]{2,1,0:T(8,128)(2,1)}, bf16[2,512,128]{2,1,0:T(8,128)(2,1)S(1)}, u32[]{:S(2)}, u32[]{:S(2)}) %collective-permute-start.3) | collective-permute-done | bytes 262176 | tf_op jit(solution)/shard_map/ppermute | solution.py:176
  31.2 0.6 collective-permute-done.5.refs_7_
  31.8 1.5 %collective-permute-start.12 = (bf16[2,512,128]{2,1,0:T(8,128)(2,1)S(1)}, bf16[2,512,128]{2,1,0:T(8,128)(2,1)S(1)}, u32[]{:S(2)}, u32[]{:S(2)}) collective-permute-start(bf16[2,512,128]{2,1,0:T(8,128)(2,1)S(1)} %collective-permute-done.4.refs_6_), channel_id=1, source_target_pairs={{0,8},{4,12},{8,0},{12,4},{1,9},{5,13},{9,1},{13,5},{2,10},{6,14},... | collective-permute-start | bytes 786440 | tf_op jit(solution)/shard_map/ppermute | solution.py:180
  33.5 0.5 collective-permute-start.13
  34.0 0.2 select_reduce_fusion.5
  34.1 6.3 %collective-permute-done.11.refs_13_ = bf16[2,512,128]{2,1,0:T(8,128)(2,1)S(1)} collective-permute-done((bf16[2,512,128]{2,1,0:T(8,128)(2,1)S(1)}, bf16[2,512,128]{2,1,0:T(8,128)(2,1)S(1)}, u32[]{:S(2)}, u32[]{:S(2)}) %collective-permute-start.11) | collective-permute-done | bytes 262176 | tf_op jit(solution)/shard_map/ppermute | solution.py:180
  40.5 0.5 collective-permute-start.14
  41.0 5.1 %collective-permute-done.12.refs_14_ = bf16[2,512,128]{2,1,0:T(8,128)(2,1)S(1)} collective-permute-done((bf16[2,512,128]{2,1,0:T(8,128)(2,1)S(1)}, bf16[2,512,128]{2,1,0:T(8,128)(2,1)S(1)}, u32[]{:S(2)}, u32[]{:S(2)}) %collective-permute-start.12) | collective-permute-done | bytes 262176 | tf_op jit(solution)/shard_map/ppermute | solution.py:180
  46.1 0.5 collective-permute-start.16
  46.6 3.2 %collective-permute-done.13.refs_15_ = bf16[2,512,128]{2,1,0:T(8,128)(2,1)S(1)} collective-permute-done((bf16[2,512,128]{2,1,0:T(8,128)(2,1)S(1)}, bf16[2,512,128]{2,1,0:T(8,128)(2,1)S(1)}, u32[]{:S(2)}, u32[]{:S(2)}) %collective-permute-start.13) | collective-permute-done | bytes 262176 | tf_op jit(solution)/shard_map/ppermute | solution.py:180
  49.7 0.2 select_reduce_fusion.4
  50.0 1.2 %collective-permute-done.17.refs_19_ = bf16[2,512,128]{2,1,0:T(8,128)(2,1)S(1)} collective-permute-done((bf16[2,512,128]{2,1,0:T(8,128)(2,1)S(1)}, bf16[2,512,128]{2,1,0:T(8,128)(2,1)S(1)}, u32[]{:S(2)}, u32[]{:S(2)}) %collective-permute-start.17) | collective-permute-done | bytes 262176 | tf_op jit(solution)/shard_map/ppermute | solution.py:180
  51.3 0.9 %copy-done = bf16[2,512,128]{2,1,0:T(8,128)(2,1)S(1)} copy-done((bf16[2,512,128]{2,1,0:T(8,128)(2,1)S(1)}, bf16[2,512,128]{2,1,0:T(8,128)(2,1)}, u32[]{:S(2)}) %copy-start) | copy-done | bytes 262168
  52.2 0.9 %copy-done.1 = bf16[128,640]{1,0:T(8,128)(2,1)S(1)} copy-done((bf16[128,640]{1,0:T(8,128)(2,1)S(1)}, bf16[128,640]{1,0:T(8,128)(2,1)}, u32[]{:S(2)}) %copy-start.1) | copy-done | bytes 163864
  53.1 12.2 %attend.1 = (bf16[128,640]{1,0:T(8,128)(2,1)S(1)}, bf16[128,640]{1,0:T(8,128)(2,1)S(1)}, bf16[128,640]{1,0:T(8,128)(2,1)S(1)}, bf16[128,640]{1,0:T(8,128)(2,1)S(1)}) custom-call(s32[4,64]{1,0:T(4,128)S(1)} %fusion.1.slots_ref, s32[4]{0:T(128)S(1)} %broadcast_add_fusion.counts_ref, bf16[128,640]{1,0:T(8,128)(2,1)S(1)} %copy-done.1, ...), custom_call_target="tpu_custom_call" | custom-call | flops 1000000000 | bytes 6000000 | tf_op jit(solution)/shard_map/attend/pallas_call | solution.py:139
  65.4 0.7 copy-done.2
  66.0 2.0 %collective-permute-start.20 = (bf16[128,640]{1,0:T(8,128)(2,1)S(1)}, bf16[128,640]{1,0:T(8,128)(2,1)S(1)}, u32[]{:S(2)}, u32[]{:S(2)}) collective-permute-start(bf16[128,640]{1,0:T(8,128)(2,1)S(1)} %get-tuple-element.28), channel_id=1, source_target_pairs={{0,1},{1,2},{2,3},{3,0},{4,5},{5,6},{6,7},{7,4},{8,9},{9,10},{10,1... | collective-permute-start | bytes 491528 | tf_op jit(solution)/shard_map/ppermute | solution.py:176
  68.0 4.0 %collective-permute-done.18.refs_1_ = bf16[128,640]{1,0:T(8,128)(2,1)S(1)} collective-permute-done((bf16[128,640]{1,0:T(8,128)(2,1)S(1)}, bf16[128,640]{1,0:T(8,128)(2,1)S(1)}, u32[]{:S(2)}, u32[]{:S(2)}) %collective-permute-start.18) | collective-permute-done | bytes 163872 | tf_op jit(solution)/shard_map/ppermute | solution.py:176
  72.0 1.6 %collective-permute-done.19.refs_2_ = bf16[128,640]{1,0:T(8,128)(2,1)S(1)} collective-permute-done((bf16[128,640]{1,0:T(8,128)(2,1)S(1)}, bf16[128,640]{1,0:T(8,128)(2,1)S(1)}, u32[]{:S(2)}, u32[]{:S(2)}) %collective-permute-start.19) | collective-permute-done | bytes 163872 | tf_op jit(solution)/shard_map/ppermute | solution.py:176
  73.6 4.4 %collective-permute-done.20.refs_3_ = bf16[128,640]{1,0:T(8,128)(2,1)S(1)} collective-permute-done((bf16[128,640]{1,0:T(8,128)(2,1)S(1)}, bf16[128,640]{1,0:T(8,128)(2,1)S(1)}, u32[]{:S(2)}, u32[]{:S(2)}) %collective-permute-start.20) | collective-permute-done | bytes 163872 | tf_op jit(solution)/shard_map/ppermute | solution.py:176
  78.0 0.7 copy-done.5
  78.7 2.1 %unpack.1 = bf16[128,2560]{1,0:T(8,128)(2,1)} custom-call(bf16[128,640]{1,0:T(8,128)(2,1)} %copy-done.2, bf16[128,640]{1,0:T(8,128)(2,1)} %copy-done.3, bf16[128,640]{1,0:T(8,128)(2,1)} %copy-done.4, bf16[128,640]{1,0:T(8,128)(2,1)} %copy-done.5), custom_call_target="tpu_custom_call" | custom-call | tf_op jit(solution)/shard_map/unpack/pallas_call | solution.py:58
  (41 shorter events, 0.5 us)
Async XLA Ops:
  2.8 30.5 %collective-permute-start.10 = (bf16[2,512,128]{2,1,0:T(8,128)(2,1)}, bf16[2,512,128]{2,1,0:T(8,128)(2,1)S(1)}, u32[]{:S(2)}, u32[]{:S(2)}) collective-permute-start(bf16[2,512,128]{2,1,0:T(8,128)(2,1)} %get-tuple-element.21.refs_4_), channel_id=1, source_target_pairs={{0,8},{4,12},{8,0},{12,4},{1,9},{5,13},{9,1},{13,5},{2,10},{6,14},... | collective-permute-start | bytes 786440 | tf_op jit(solution)/shard_map/ppermute | solution.py:180
  5.1 28.4 %collective-permute-start.6 = (bf16[2,512,128]{2,1,0:T(8,128)(2,1)}, bf16[2,512,128]{2,1,0:T(8,128)(2,1)S(1)}, u32[]{:S(2)}, u32[]{:S(2)}) collective-permute-start(bf16[2,512,128]{2,1,0:T(8,128)(2,1)} %get-tuple-element.21.refs_4_), channel_id=1, source_target_pairs={{0,4},{4,0},{8,12},{12,8},{1,5},{5,1},{9,13},{13,9},{2,6},{6,2},{1... | collective-permute-start | bytes 786440 | tf_op jit(solution)/shard_map/ppermute | solution.py:180
  5.1 11.5 %collective-permute-start = (bf16[128,640]{1,0:T(8,128)(2,1)}, bf16[128,640]{1,0:T(8,128)(2,1)S(1)}, u32[]{:S(2)}, u32[]{:S(2)}) collective-permute-start(bf16[128,640]{1,0:T(8,128)(2,1)} %get-tuple-element.18), channel_id=1, source_target_pairs={{0,1},{1,2},{2,3},{3,0},{4,5},{5,6},{6,7},{7,4},{8,9},{9,10},{10,1... | collective-permute-start | bytes 491528 | tf_op jit(solution)/shard_map/ppermute | solution.py:176
  5.1 11.5 %collective-permute-start.1 = (bf16[128,640]{1,0:T(8,128)(2,1)}, bf16[128,640]{1,0:T(8,128)(2,1)S(1)}, u32[]{:S(2)}, u32[]{:S(2)}) collective-permute-start(bf16[128,640]{1,0:T(8,128)(2,1)} %get-tuple-element.19), channel_id=1, source_target_pairs={{0,2},{1,3},{2,0},{3,1},{4,6},{5,7},{6,4},{7,5},{8,10},{9,11},{10,... | collective-permute-start | bytes 491528 | tf_op jit(solution)/shard_map/ppermute | solution.py:176
  7.8 9.8 %collective-permute-start.2 = (bf16[128,640]{1,0:T(8,128)(2,1)}, bf16[128,640]{1,0:T(8,128)(2,1)S(1)}, u32[]{:S(2)}, u32[]{:S(2)}) collective-permute-start(bf16[128,640]{1,0:T(8,128)(2,1)} %get-tuple-element.20), channel_id=1, source_target_pairs={{0,3},{1,0},{2,1},{3,2},{4,7},{5,4},{6,5},{7,6},{8,11},{9,8},{10,9... | collective-permute-start | bytes 491528 | tf_op jit(solution)/shard_map/ppermute | solution.py:176
  9.2 0.7 copy-start.6
  16.6 14.6 %collective-permute-start.3 = (bf16[2,512,128]{2,1,0:T(8,128)(2,1)}, bf16[2,512,128]{2,1,0:T(8,128)(2,1)S(1)}, u32[]{:S(2)}, u32[]{:S(2)}) collective-permute-start(bf16[2,512,128]{2,1,0:T(8,128)(2,1)} %get-tuple-element.22), channel_id=1, source_target_pairs={{0,1},{1,2},{2,3},{3,0},{4,5},{5,6},{6,7},{7,4},{8,9},{9,10},{10,1... | collective-permute-start | bytes 786440 | tf_op jit(solution)/shard_map/ppermute | solution.py:176
  16.6 14.6 %collective-permute-start.4 = (bf16[2,512,128]{2,1,0:T(8,128)(2,1)}, bf16[2,512,128]{2,1,0:T(8,128)(2,1)S(1)}, u32[]{:S(2)}, u32[]{:S(2)}) collective-permute-start(bf16[2,512,128]{2,1,0:T(8,128)(2,1)} %get-tuple-element.23), channel_id=1, source_target_pairs={{0,2},{1,3},{2,0},{3,1},{4,6},{5,7},{6,4},{7,5},{8,10},{9,11},{10,... | collective-permute-start | bytes 786440 | tf_op jit(solution)/shard_map/ppermute | solution.py:176
  17.7 14.2 %collective-permute-start.5 = (bf16[2,512,128]{2,1,0:T(8,128)(2,1)}, bf16[2,512,128]{2,1,0:T(8,128)(2,1)S(1)}, u32[]{:S(2)}, u32[]{:S(2)}) collective-permute-start(bf16[2,512,128]{2,1,0:T(8,128)(2,1)} %get-tuple-element.24), channel_id=1, source_target_pairs={{0,3},{1,0},{2,1},{3,2},{4,7},{5,4},{6,5},{7,6},{8,11},{9,8},{10,9... | collective-permute-start | bytes 786440 | tf_op jit(solution)/shard_map/ppermute | solution.py:176
  20.1 13.9 %copy-start.7 = (s32[16]{0:T(128)S(1)}, s32[16]{0:T(128)}, u32[]{:S(2)}) copy-start(s32[16]{0:T(128)} %param.9) | copy-start | bytes 196
  31.2 9.2 %collective-permute-start.11 = (bf16[2,512,128]{2,1,0:T(8,128)(2,1)S(1)}, bf16[2,512,128]{2,1,0:T(8,128)(2,1)S(1)}, u32[]{:S(2)}, u32[]{:S(2)}) collective-permute-start(bf16[2,512,128]{2,1,0:T(8,128)(2,1)S(1)} %collective-permute-done.3.refs_5_), channel_id=1, source_target_pairs={{0,8},{4,12},{8,0},{12,4},{1,9},{5,13},{9,1},{13,5},{2,10},{6,14},... | collective-permute-start | bytes 786440 | tf_op jit(solution)/shard_map/ppermute | solution.py:180
  31.2 9.2 %collective-permute-start.7 = (bf16[2,512,128]{2,1,0:T(8,128)(2,1)S(1)}, bf16[2,512,128]{2,1,0:T(8,128)(2,1)S(1)}, u32[]{:S(2)}, u32[]{:S(2)}) collective-permute-start(bf16[2,512,128]{2,1,0:T(8,128)(2,1)S(1)} %collective-permute-done.3.refs_5_), channel_id=1, source_target_pairs={{0,4},{4,0},{8,12},{12,8},{1,5},{5,1},{9,13},{13,9},{2,6},{6,2},{1... | collective-permute-start | bytes 786440 | tf_op jit(solution)/shard_map/ppermute | solution.py:180
  31.8 14.2 %collective-permute-start.12 = (bf16[2,512,128]{2,1,0:T(8,128)(2,1)S(1)}, bf16[2,512,128]{2,1,0:T(8,128)(2,1)S(1)}, u32[]{:S(2)}, u32[]{:S(2)}) collective-permute-start(bf16[2,512,128]{2,1,0:T(8,128)(2,1)S(1)} %collective-permute-done.4.refs_6_), channel_id=1, source_target_pairs={{0,8},{4,12},{8,0},{12,4},{1,9},{5,13},{9,1},{13,5},{2,10},{6,14},... | collective-permute-start | bytes 786440 | tf_op jit(solution)/shard_map/ppermute | solution.py:180
  33.3 12.7 %collective-permute-start.8 = (bf16[2,512,128]{2,1,0:T(8,128)(2,1)S(1)}, bf16[2,512,128]{2,1,0:T(8,128)(2,1)S(1)}, u32[]{:S(2)}, u32[]{:S(2)}) collective-permute-start(bf16[2,512,128]{2,1,0:T(8,128)(2,1)S(1)} %collective-permute-done.4.refs_6_), channel_id=1, source_target_pairs={{0,4},{4,0},{8,12},{12,8},{1,5},{5,1},{9,13},{13,9},{2,6},{6,2},{1... | collective-permute-start | bytes 786440 | tf_op jit(solution)/shard_map/ppermute | solution.py:180
  33.5 16.2 %collective-permute-start.13 = (bf16[2,512,128]{2,1,0:T(8,128)(2,1)S(1)}, bf16[2,512,128]{2,1,0:T(8,128)(2,1)S(1)}, u32[]{:S(2)}, u32[]{:S(2)}) collective-permute-start(bf16[2,512,128]{2,1,0:T(8,128)(2,1)S(1)} %collective-permute-done.5.refs_7_), channel_id=1, source_target_pairs={{0,8},{4,12},{8,0},{12,4},{1,9},{5,13},{9,1},{13,5},{2,10},{6,14},... | collective-permute-start | bytes 786440 | tf_op jit(solution)/shard_map/ppermute | solution.py:180
  40.4 9.6 %collective-permute-start.9 = (bf16[2,512,128]{2,1,0:T(8,128)(2,1)S(1)}, bf16[2,512,128]{2,1,0:T(8,128)(2,1)S(1)}, u32[]{:S(2)}, u32[]{:S(2)}) collective-permute-start(bf16[2,512,128]{2,1,0:T(8,128)(2,1)S(1)} %collective-permute-done.5.refs_7_), channel_id=1, source_target_pairs={{0,4},{4,0},{8,12},{12,8},{1,5},{5,1},{9,13},{13,9},{2,6},{6,2},{1... | collective-permute-start | bytes 786440 | tf_op jit(solution)/shard_map/ppermute | solution.py:180
  40.5 9.6 %collective-permute-start.14 = (bf16[2,512,128]{2,1,0:T(8,128)(2,1)S(1)}, bf16[2,512,128]{2,1,0:T(8,128)(2,1)S(1)}, u32[]{:S(2)}, u32[]{:S(2)}) collective-permute-start(bf16[2,512,128]{2,1,0:T(8,128)(2,1)S(1)} %collective-permute-done.10.refs_12_), channel_id=1, source_target_pairs={{0,4},{4,0},{8,12},{12,8},{1,5},{5,1},{9,13},{13,9},{2,6},{6,2},{1... | collective-permute-start | bytes 786440 | tf_op jit(solution)/shard_map/ppermute | solution.py:180
  46.1 3.9 %collective-permute-start.15 = (bf16[2,512,128]{2,1,0:T(8,128)(2,1)S(1)}, bf16[2,512,128]{2,1,0:T(8,128)(2,1)S(1)}, u32[]{:S(2)}, u32[]{:S(2)}) collective-permute-start(bf16[2,512,128]{2,1,0:T(8,128)(2,1)S(1)} %collective-permute-done.11.refs_13_), channel_id=1, source_target_pairs={{0,4},{4,0},{8,12},{12,8},{1,5},{5,1},{9,13},{13,9},{2,6},{6,2},{1... | collective-permute-start | bytes 786440 | tf_op jit(solution)/shard_map/ppermute | solution.py:180
  46.1 3.9 %collective-permute-start.16 = (bf16[2,512,128]{2,1,0:T(8,128)(2,1)S(1)}, bf16[2,512,128]{2,1,0:T(8,128)(2,1)S(1)}, u32[]{:S(2)}, u32[]{:S(2)}) collective-permute-start(bf16[2,512,128]{2,1,0:T(8,128)(2,1)S(1)} %collective-permute-done.12.refs_14_), channel_id=1, source_target_pairs={{0,4},{4,0},{8,12},{12,8},{1,5},{5,1},{9,13},{13,9},{2,6},{6,2},{1... | collective-permute-start | bytes 786440 | tf_op jit(solution)/shard_map/ppermute | solution.py:180
  49.7 1.5 %collective-permute-start.17 = (bf16[2,512,128]{2,1,0:T(8,128)(2,1)S(1)}, bf16[2,512,128]{2,1,0:T(8,128)(2,1)S(1)}, u32[]{:S(2)}, u32[]{:S(2)}) collective-permute-start(bf16[2,512,128]{2,1,0:T(8,128)(2,1)S(1)} %collective-permute-done.13.refs_15_), channel_id=1, source_target_pairs={{0,4},{4,0},{8,12},{12,8},{1,5},{5,1},{9,13},{13,9},{2,6},{6,2},{1... | collective-permute-start | bytes 786440 | tf_op jit(solution)/shard_map/ppermute | solution.py:180
  51.3 1.0 %copy-start = (bf16[2,512,128]{2,1,0:T(8,128)(2,1)S(1)}, bf16[2,512,128]{2,1,0:T(8,128)(2,1)}, u32[]{:S(2)}) copy-start(bf16[2,512,128]{2,1,0:T(8,128)(2,1)} %get-tuple-element.21.refs_4_) | copy-start | bytes 786436
  52.2 0.9 %copy-start.1 = (bf16[128,640]{1,0:T(8,128)(2,1)S(1)}, bf16[128,640]{1,0:T(8,128)(2,1)}, u32[]{:S(2)}) copy-start(bf16[128,640]{1,0:T(8,128)(2,1)} %get-tuple-element.17.refs_0_) | copy-start | bytes 491524
  65.3 0.7 copy-start.2
  66.0 6.0 %collective-permute-start.18 = (bf16[128,640]{1,0:T(8,128)(2,1)S(1)}, bf16[128,640]{1,0:T(8,128)(2,1)S(1)}, u32[]{:S(2)}, u32[]{:S(2)}) collective-permute-start(bf16[128,640]{1,0:T(8,128)(2,1)S(1)} %get-tuple-element.26), channel_id=1, source_target_pairs={{0,3},{1,0},{2,1},{3,2},{4,7},{5,4},{6,5},{7,6},{8,11},{9,8},{10,9... | collective-permute-start | bytes 491528 | tf_op jit(solution)/shard_map/ppermute | solution.py:176
  66.0 7.6 %collective-permute-start.19 = (bf16[128,640]{1,0:T(8,128)(2,1)S(1)}, bf16[128,640]{1,0:T(8,128)(2,1)S(1)}, u32[]{:S(2)}, u32[]{:S(2)}) collective-permute-start(bf16[128,640]{1,0:T(8,128)(2,1)S(1)} %get-tuple-element.27), channel_id=1, source_target_pairs={{0,2},{1,3},{2,0},{3,1},{4,6},{5,7},{6,4},{7,5},{8,10},{9,11},{10,... | collective-permute-start | bytes 491528 | tf_op jit(solution)/shard_map/ppermute | solution.py:176
  66.0 12.0 %collective-permute-start.20 = (bf16[128,640]{1,0:T(8,128)(2,1)S(1)}, bf16[128,640]{1,0:T(8,128)(2,1)S(1)}, u32[]{:S(2)}, u32[]{:S(2)}) collective-permute-start(bf16[128,640]{1,0:T(8,128)(2,1)S(1)} %get-tuple-element.28), channel_id=1, source_target_pairs={{0,1},{1,2},{2,3},{3,0},{4,5},{5,6},{6,7},{7,4},{8,9},{9,10},{10,1... | collective-permute-start | bytes 491528 | tf_op jit(solution)/shard_map/ppermute | solution.py:176
  72.0 6.0 %copy-start.3 = (bf16[128,640]{1,0:T(8,128)(2,1)}, bf16[128,640]{1,0:T(8,128)(2,1)S(1)}, u32[]{:S(2)}) copy-start(bf16[128,640]{1,0:T(8,128)(2,1)S(1)} %collective-permute-done.18.refs_1_) | copy-start | bytes 491524
  73.6 4.4 %copy-start.4 = (bf16[128,640]{1,0:T(8,128)(2,1)}, bf16[128,640]{1,0:T(8,128)(2,1)S(1)}, u32[]{:S(2)}) copy-start(bf16[128,640]{1,0:T(8,128)(2,1)S(1)} %collective-permute-done.19.refs_2_) | copy-start | bytes 491524
  78.0 0.7 copy-start.5
